TPU v7x, 32 devices: a whole 2x2x4 slice. The times are simulated.
32 devices in a mesh: seq: 8 (over z, y), pb: 4 (over x, core).
Axes of the slice: x: 2, y: 2, z: 4, core: 2. Of those that a mesh axis runs over, the one named last changes fastest.
Arguments:
- tokens: bfloat16 [2048, 2048], P('seq'), may hold values from -0.119628906 to 0.119628906
- w_query: bfloat16 [2048, 2048], P(None, 'pb')
- w_key: bfloat16 [2048, 2048], P(None, 'pb')
- w_value: bfloat16 [2048, 2048], P(None, 'pb'), may hold values from -0.125 to 0.125
- w_out: bfloat16 [2048, 2048], P('pb'), may hold values from -0.125 to 0.125
- gain_attn: float32 [2048], replicated, may hold values from 0.1 to 1.9
- gain_embed: float32 [2048], replicated, may hold values from 0.1 to 1.9
- queries: bfloat16 [32, 32, 2048], P(('seq', 'pb')), may hold values from -0.125 to 0.125
- query_lengths: int32 [32], P(('seq', 'pb')), may hold values from 8 to 32
- group_lengths: int32 [16], replicated, may hold values from 1 to 1024, 2048 in all
- teacher: float32 [32, 16], P(('seq', 'pb')), may hold values from -12 to 12
Outputs:
- embedded: bfloat16 [2048, 2048], P('seq')
- scores: float32 [32, 16], P(('seq', 'pb'))
- score_gradient: float32 [32, 16], P(('seq', 'pb'))
- distill_loss: float32 [], replicated
Inputs may be any that keep to these rules, and one draw needn't show every extreme that they name: `group_lengths`: the groups cover the document in order: the lengths sum to 2048.
All inputs are finite; a program needn't handle non-finite values.
Results may differ from a plain program's by a relative error of at most 0.013.
Values may be sent and summed in bfloat16 or wider, within the bound.
A program may use at most 128 MiB of HBM per device.

v0:
```python
import jax
import jax.numpy as jnp
from jax import lax
from jax.sharding import PartitionSpec as P

HD = 128
WIN = 2048
LQ = 32


EPSILON = 1e-06
SOFTMAX_TEMP = 0.1


def shifted_2(x, axis, by):
    count = lax.axis_size(axis)
    pairs = [(i, i + by) for i in range(count) if 0 <= i + by < count]
    return lax.ppermute(x, axis, pairs)


def rms_scale(values, gain):
    mean_sq = jnp.mean(values * values, axis=-1, keepdims=True)
    return values * lax.rsqrt(mean_sq + EPSILON) * gain


def segmented_max(values, group_id):
    span_len = values.shape[-1]
    stride = 1
    while stride < span_len:
        filler = jnp.full(values.shape[:-1] + (stride,), -jnp.inf, values.dtype)
        shifted = jnp.concatenate([filler, values[..., :-stride]], axis=-1)
        prior_id = jnp.concatenate([jnp.full((stride,), -1, jnp.int32), group_id[:-stride]])
        values = jnp.where((prior_id == group_id)[None, :], jnp.maximum(values, shifted), values)
        stride = stride * 2
    return values


def per_device(
    tokens,
    w_query,
    w_key,
    w_value,
    w_out,
    gain_attn,
    gain_embed,
    queries,
    query_lengths,
    group_lengths,
    teacher,
):
    shard_rows = tokens.shape[0]
    seq_count = lax.axis_size("seq")
    seq_place = lax.axis_index("seq")
    head_width = w_query.shape[1]
    heads_here = head_width // HD
    half_win = WIN // 2
    reach_count = half_win // shard_rows
    my_start = seq_place * shard_rows
    total_tokens = shard_rows * seq_count
    residual = tokens.astype(jnp.float32)
    normed = rms_scale(residual, gain_attn).astype(jnp.bfloat16)
    q_local = jnp.dot(normed, w_query, preferred_element_type=jnp.float32).astype(jnp.bfloat16)
    k_local = jnp.dot(normed, w_key, preferred_element_type=jnp.float32).astype(jnp.bfloat16)
    v_local = jnp.dot(normed, w_value, preferred_element_type=jnp.float32).astype(jnp.bfloat16)
    key_value = jnp.stack([k_local, v_local])
    earlier = [shifted_2(key_value, "seq", distance) for distance in range(reach_count, 0, -1)]
    later = [shifted_2(key_value, "seq", -distance) for distance in range(1, reach_count + 1)]
    window = jnp.concatenate(earlier + [key_value] + later, axis=1)
    span_rows = window.shape[1]
    q_pos = my_start + jnp.arange(shard_rows, dtype=jnp.int32)
    k_pos = my_start - reach_count * shard_rows + jnp.arange(span_rows, dtype=jnp.int32)
    in_window = (
        (jnp.abs(q_pos[:, None] - k_pos[None, :]) <= half_win)
        & (k_pos >= 0)[None, :]
        & (k_pos < total_tokens)[None, :]
    )
    q_heads = q_local.reshape(shard_rows, heads_here, HD)
    k_heads = window[0].reshape(span_rows, heads_here, HD)
    v_heads = window[1].reshape(span_rows, heads_here, HD)
    logits = jnp.einsum(
        "qhd,khd->hqk", q_heads, k_heads, preferred_element_type=jnp.float32
    ) * HD ** (-0.5)
    logits = jnp.where(in_window[None], logits, -jnp.inf)
    row_max = jnp.max(logits, axis=-1, keepdims=True)
    exp_terms = jnp.exp(logits - row_max)
    weights = (exp_terms / jnp.sum(exp_terms, axis=-1, keepdims=True)).astype(jnp.bfloat16)
    mixed = jnp.einsum("hqk,khd->qhd", weights, v_heads, preferred_element_type=jnp.float32)
    mixed = mixed.reshape(shard_rows, head_width).astype(jnp.bfloat16)
    partial_value = jnp.dot(mixed, w_out, preferred_element_type=jnp.float32)
    attn_sum = lax.psum(partial_value, "pb")
    embedded = rms_scale(residual + attn_sum, gain_embed).astype(jnp.bfloat16)
    group_end = jnp.cumsum(group_lengths)
    group_start = group_end - group_lengths
    group_id = jnp.sum((group_end[None, :] <= q_pos[:, None]).astype(jnp.int32), axis=1)
    last_local = jnp.clip(group_end - 1 - my_start, 0, shard_rows - 1)
    present = (group_start < my_start + shard_rows) & (group_end > my_start)
    q_piece = lax.all_gather(queries, "seq", axis=0, tiled=True)
    count = q_piece.shape[0]
    q_rows = q_piece.reshape(count * q_piece.shape[1], q_piece.shape[2])
    similar = jnp.einsum("td,rd->tr", q_rows, embedded, preferred_element_type=jnp.float32)
    running = segmented_max(similar, group_id)
    picked = jnp.take(running, last_local, axis=1)
    picked = jnp.where(present[None, :], picked, -jnp.inf)
    part_max = picked.reshape(count, q_piece.shape[1], picked.shape[-1])
    own_count = queries.shape[0]
    all_maxima = lax.pmax(part_max, "seq")
    token_max = lax.dynamic_slice_in_dim(all_maxima, seq_place * own_count, own_count, 0)
    live_mask = (jnp.arange(LQ, dtype=jnp.int32)[None, :] < query_lengths[:, None]).astype(
        jnp.float32
    )
    scores = (
        jnp.sum(token_max * live_mask[:, :, None], axis=1)
        / query_lengths.astype(jnp.float32)[:, None]
    )
    student_scores = scores / SOFTMAX_TEMP
    student_scores = student_scores - jnp.max(student_scores, axis=-1, keepdims=True)
    student_log_prob = student_scores - jnp.log(
        jnp.sum(jnp.exp(student_scores), axis=-1, keepdims=True)
    )
    target_scores = teacher / SOFTMAX_TEMP
    target_scores = target_scores - jnp.max(target_scores, axis=-1, keepdims=True)
    log_t = target_scores - jnp.log(jnp.sum(jnp.exp(target_scores), axis=-1, keepdims=True))
    teacher_prob = jnp.exp(log_t)
    kl_terms = jnp.sum(teacher_prob * (log_t - student_log_prob), axis=-1)
    query_count_all = own_count * seq_count * lax.axis_size("pb")
    distill_loss = lax.psum(jnp.sum(kl_terms), ("seq", "pb")) / query_count_all
    score_gradient = (jnp.exp(student_log_prob) - teacher_prob) / (SOFTMAX_TEMP * query_count_all)
    return (embedded, scores, score_gradient, distill_loss)


def solution(mesh):
    placed = (
        P("seq", None),
        P(None, "pb"),
        P(None, "pb"),
        P(None, "pb"),
        P("pb", None),
        P(),
        P(),
        P(("seq", "pb"), None, None),
        P(("seq", "pb")),
        P(),
        P(("seq", "pb"), None),
    )
    return jax.shard_map(
        per_device,
        mesh=mesh,
        in_specs=placed,
        out_specs=(P("seq", None), P(("seq", "pb"), None), P(("seq", "pb"), None), P()),
        check_vma=False,
    )
```

profile of v0, /device:TPU:0, one launch (start us, length us, event | category | flops | bytes accessed | tf_op | source)
XLA Modules:
  0.0 284.1 jit_solution(10187921965544710058)
XLA Ops:
  8.1 1.6 fusion.10
  9.8 2.8 fusion.15
  12.6 0.8 fusion.14
  13.4 0.7 copy-done.3
  14.1 0.8 pad_maximum_fusion
  14.9 6.7 %collective-permute-start = (bf16[2,256,512]{2,1,0:T(8,128)(2,1)}, bf16[2,256,512]{2,1,0:T(8,128)(2,1)}, u32[]{:S(2)}, u32[]{:S(2)}) collective-permute-start(bf16[2,256,512]{2,1,0:T(8,128)(2,1)} %pad_maximum_fusion), channel_id=1, source_target_pairs={{0,16},{4,20},{8,24},{12,28},{1,17},{5,21},{9,25},{13,29},{2,18},{... | collective-permute-start | bytes 1572872 | tf_op jit(solution)/shard_map/ppermute | solution.py:18
  21.7 5.2 %collective-permute-start.1 = (bf16[2,256,512]{2,1,0:T(8,128)(2,1)}, bf16[2,256,512]{2,1,0:T(8,128)(2,1)}, u32[]{:S(2)}, u32[]{:S(2)}) collective-permute-start(bf16[2,256,512]{2,1,0:T(8,128)(2,1)} %pad_maximum_fusion), channel_id=1, source_target_pairs={{0,12},{4,16},{8,20},{12,24},{16,28},{1,13},{5,17},{9,21},{13,25},... | collective-permute-start | bytes 1572872 | tf_op jit(solution)/shard_map/ppermute | solution.py:18
  26.9 2.1 collective-permute-start.2
  29.0 3.1 %collective-permute-start.3 = (bf16[2,256,512]{2,1,0:T(8,128)(2,1)}, bf16[2,256,512]{2,1,0:T(8,128)(2,1)}, u32[]{:S(2)}, u32[]{:S(2)}) collective-permute-start(bf16[2,256,512]{2,1,0:T(8,128)(2,1)} %pad_maximum_fusion), channel_id=1, source_target_pairs={{0,4},{4,8},{8,12},{12,16},{16,20},{20,24},{24,28},{1,5},{5,9},{9,... | collective-permute-start | bytes 1572872 | tf_op jit(solution)/shard_map/ppermute | solution.py:18
  32.1 1.3 collective-permute-start.4
  33.5 1.7 fusion.9
  35.1 3.0 %fusion.16 = bf16[32,4,8,128]{3,2,1,0:T(8,128)(2,1)} fusion(bf16[2048,512]{1,0:T(8,128)(2,1)} %param.12, bf16[256,2048]{1,0:T(8,128)(2,1)S(1)} %copy-done.1, f32[2048]{0:T(1024)S(1)} %copy-done.10, f32[256]{0:T(256)S(1)} %add_rsqrt_fusion.1), kind=kOutput, calls=%fused_computation.29 | convolution fusion | flops 539099136 | bytes 3417088 | tf_op jit(solution)/shard_map/dot_general | solution.py:62
  38.2 1.4 collective-permute-start.5
  39.6 1.1 constant_dynamic-update-slice_fusion.8
  40.7 12.7 %collective-permute-done.1 = bf16[2,256,512]{2,1,0:T(8,128)(2,1)} collective-permute-done((bf16[2,256,512]{2,1,0:T(8,128)(2,1)}, bf16[2,256,512]{2,1,0:T(8,128)(2,1)}, u32[]{:S(2)}, u32[]{:S(2)}) %collective-permute-start.1) | collective-permute-done | bytes 524320 | tf_op jit(solution)/shard_map/ppermute | solution.py:18
  53.4 1.3 collective-permute-start.6
  54.6 1.1 constant_dynamic-update-slice_fusion.7
  55.7 7.7 %collective-permute-done.2 = bf16[2,256,512]{2,1,0:T(8,128)(2,1)} collective-permute-done((bf16[2,256,512]{2,1,0:T(8,128)(2,1)}, bf16[2,256,512]{2,1,0:T(8,128)(2,1)}, u32[]{:S(2)}, u32[]{:S(2)}) %collective-permute-start.2) | collective-permute-done | bytes 524320 | tf_op jit(solution)/shard_map/ppermute | solution.py:18
  63.4 1.3 collective-permute-start.7
  64.7 1.1 constant_dynamic-update-slice_fusion.6
  65.8 1.1 constant_dynamic-update-slice_fusion.5
  67.0 1.1 constant_dynamic-update-slice_fusion.3
  68.1 14.6 %collective-permute-done.6 = bf16[2,256,512]{2,1,0:T(8,128)(2,1)S(1)} collective-permute-done((bf16[2,256,512]{2,1,0:T(8,128)(2,1)}, bf16[2,256,512]{2,1,0:T(8,128)(2,1)S(1)}, u32[]{:S(2)}, u32[]{:S(2)}) %collective-permute-start.6) | collective-permute-done | bytes 524320 | tf_op jit(solution)/shard_map/ppermute | solution.py:18
  82.8 27.0 %collective-permute-done.7 = bf16[2,256,512]{2,1,0:T(8,128)(2,1)S(1)} collective-permute-done((bf16[2,256,512]{2,1,0:T(8,128)(2,1)}, bf16[2,256,512]{2,1,0:T(8,128)(2,1)S(1)}, u32[]{:S(2)}, u32[]{:S(2)}) %collective-permute-start.7) | collective-permute-done | bytes 524320 | tf_op jit(solution)/shard_map/ppermute | solution.py:18
  109.8 2.4 fusion.39
  112.2 4.3 %copy.31 = bf16[1,2304,512]{1,2,0:T(8,128)(2,1)} copy(bf16[1,2304,512]{2,1,0:T(8,128)(2,1)} %get-tuple-element.9) | data formatting | bytes 4718592 | tf_op jit(solution)/shard_map/reshape;squeeze | solution.py:79
  116.5 5.3 %reshape_squeeze.7 = bf16[2304,4,128]{2,1,0:T(4,128)(2,1)} reshape(bf16[1,2304,512]{2,1,0:T(8,128)(2,1)} %get-tuple-element.8) | data formatting | bytes 4718592 | tf_op jit(solution)/shard_map/reshape;squeeze | solution.py:78
  121.9 8.8 %fusion.40 = (f32[4,256]{1,0:T(4,128)S(1)}, f32[4,256,2304]{2,1,0:T(8,128)}) fusion(pred[256,2304]{1,0:T(8,128)(4,1)} %fusion.9, bf16[2304,4,128]{2,1,0:T(4,128)(2,1)} %reshape_squeeze.7, bf16[32,4,8,128]{3,2,1,0:T(8,128)(2,1)S(1)} %copy-done.11), kind=kOutput, calls=%fused_computation.89 | convolution fusion | flops 613419264 | bytes 12652544 | tf_op jit(solution)/shard_map/sub | solution.py:85
  130.6 6.2 %fusion.13 = bf16[4,128,256]{2,1,0:T(8,128)(2,1)S(1)} fusion(bf16[2304,4,128]{0,2,1:T(8,128)(2,1)} %bitcast.50, f32[4,256,2304]{2,1,0:T(8,128)} %get-tuple-element.23, f32[4,256]{1,0:T(4,128)S(1)} %get-tuple-element.22), kind=kOutput, calls=%fused_computation.23 | convolution fusion | flops 608829440 | bytes 12062720 | tf_op jit(solution)/shard_map/hqk,khd->qhd/dot_general | solution.py:87
  136.8 2.0 fusion.45
  138.9 0.2 all-gather.2.cloned.1.call-start
  139.1 0.3 all-gather.2.cloned.1.call-update
  139.6 0.1 fusion.33
  139.8 0.6 multiply_reduce_fusion.3
  141.1 1.2 exponential_reduce_fusion
  143.2 44.5 %all-reduce.17.cloned.1.call-done = f32[256,2048]{1,0:T(8,128)} async-done(((f32[256,2048]{1,0:T(8,128)}), f32[256,2048]{1,0:T(8,128)}) %all-reduce.17.cloned.1.call-update) | async-done | bytes 2097168 | tf_op jit(solution)/shard_map/psum | solution.py:90
  187.7 2.1 multiply_reduce_fusion
  189.8 0.1 copy-done.2
  189.9 1.3 multiply_convert_fusion
  191.2 2.0 convolution_bitcast_fusion
  194.2 0.6 gather_fusion
  194.8 0.1 select_select_fusion
  195.0 37.5 %pmax.7 = f32[8,32,16]{1,0,2:T(8,128)S(1)} all-reduce(f32[8,32,16]{1,0,2:T(8,128)S(1)} %select_select_fusion), channel_id=1, replica_groups=mesh['seq'=8,'pb'=4] {'seq'}, use_global_device_ids=true, to_apply=%region_7.8 | all-reduce | flops 4096 | bytes 32768 | tf_op jit(solution)/shard_map/pmax | solution.py:106
  232.5 0.2 multiply_reduce_fusion.1
  232.7 0.6 multiply_reduce_fusion.4
  233.3 1.3 exponential_reduce_fusion.1
  235.3 2.5 multiply_reduce_fusion.2
  237.7 37.1 %psum.15 = f32[]{:T(128)} all-reduce(f32[]{:T(128)} %get-tuple-element.10), channel_id=1, replica_groups=mesh['seq'=8,'pb'=4] {'seq','pb'}, use_global_device_ids=true, to_apply=%region_14.15 | all-reduce | flops 1 | bytes 8 | tf_op jit(solution)/shard_map/psum | solution.py:126
  (60 shorter events, 1.6 us)
Async XLA Ops:
  8.0 128.8 %copy-start = (bf16[512,2048]{1,0:T(8,128)(2,1)S(1)}, bf16[512,2048]{1,0:T(8,128)(2,1)}, u32[]{:S(2)}) copy-start(bf16[512,2048]{1,0:T(8,128)(2,1)} %param.15) | copy-start | bytes 6291460
  8.0 179.6 %all-reduce.17.cloned.1.call-start = ((), (), s32[]{:S(2)}) async-start(), calls=%async_computation | async-start | bytes 4194304 | tf_op jit(solution)/shard_map/psum | solution.py:90
  9.7 2.9 %copy-start.1 = (bf16[256,2048]{1,0:T(8,128)(2,1)S(1)}, bf16[256,2048]{1,0:T(8,128)(2,1)}, u32[]{:S(2)}) copy-start(bf16[256,2048]{1,0:T(8,128)(2,1)} %param.11) | copy-start | bytes 3145732
  9.7 2.9 %copy-start.9 = (bf16[2048,512]{1,0:T(8,128)(2,1)S(1)}, bf16[2048,512]{1,0:T(8,128)(2,1)}, u32[]{:S(2)}) copy-start(bf16[2048,512]{1,0:T(8,128)(2,1)} %param.13) | copy-start | bytes 6291460
  9.7 2.9 %copy-start.10 = (f32[2048]{0:T(1024)S(1)}, f32[2048]{0:T(1024)}, u32[]{:S(2)}) copy-start(f32[2048]{0:T(1024)} %param.16) | copy-start | bytes 24580
  13.4 0.7 copy-start.3
  14.9 23.2 %collective-permute-start = (bf16[2,256,512]{2,1,0:T(8,128)(2,1)}, bf16[2,256,512]{2,1,0:T(8,128)(2,1)}, u32[]{:S(2)}, u32[]{:S(2)}) collective-permute-start(bf16[2,256,512]{2,1,0:T(8,128)(2,1)} %pad_maximum_fusion), channel_id=1, source_target_pairs={{0,16},{4,20},{8,24},{12,28},{1,17},{5,21},{9,25},{13,29},{2,18},{... | collective-permute-start | bytes 1572872 | tf_op jit(solution)/shard_map/ppermute | solution.py:18
  21.7 31.7 %collective-permute-start.1 = (bf16[2,256,512]{2,1,0:T(8,128)(2,1)}, bf16[2,256,512]{2,1,0:T(8,128)(2,1)}, u32[]{:S(2)}, u32[]{:S(2)}) collective-permute-start(bf16[2,256,512]{2,1,0:T(8,128)(2,1)} %pad_maximum_fusion), channel_id=1, source_target_pairs={{0,12},{4,16},{8,20},{12,24},{16,28},{1,13},{5,17},{9,21},{13,25},... | collective-permute-start | bytes 1572872 | tf_op jit(solution)/shard_map/ppermute | solution.py:18
  26.9 36.5 %collective-permute-start.2 = (bf16[2,256,512]{2,1,0:T(8,128)(2,1)}, bf16[2,256,512]{2,1,0:T(8,128)(2,1)}, u32[]{:S(2)}, u32[]{:S(2)}) collective-permute-start(bf16[2,256,512]{2,1,0:T(8,128)(2,1)} %pad_maximum_fusion), channel_id=1, source_target_pairs={{0,8},{4,12},{8,16},{12,20},{16,24},{20,28},{1,9},{5,13},{9,17},{1... | collective-permute-start | bytes 1572872 | tf_op jit(solution)/shard_map/ppermute | solution.py:18
  29.0 36.8 %collective-permute-start.3 = (bf16[2,256,512]{2,1,0:T(8,128)(2,1)}, bf16[2,256,512]{2,1,0:T(8,128)(2,1)}, u32[]{:S(2)}, u32[]{:S(2)}) collective-permute-start(bf16[2,256,512]{2,1,0:T(8,128)(2,1)} %pad_maximum_fusion), channel_id=1, source_target_pairs={{0,4},{4,8},{8,12},{12,16},{16,20},{20,24},{24,28},{1,5},{5,9},{9,... | collective-permute-start | bytes 1572872 | tf_op jit(solution)/shard_map/ppermute | solution.py:18
  32.1 34.8 %collective-permute-start.4 = (bf16[2,256,512]{2,1,0:T(8,128)(2,1)}, bf16[2,256,512]{2,1,0:T(8,128)(2,1)}, u32[]{:S(2)}, u32[]{:S(2)}) collective-permute-start(bf16[2,256,512]{2,1,0:T(8,128)(2,1)} %pad_maximum_fusion), channel_id=1, source_target_pairs={{4,0},{8,4},{12,8},{16,12},{20,16},{24,20},{28,24},{5,1},{9,5},{13... | collective-permute-start | bytes 1572872 | tf_op jit(solution)/shard_map/ppermute | solution.py:18
  38.2 28.7 %copy-start.4 = (bf16[1,256,512]{2,1,0:T(8,128)(2,1)S(1)}, bf16[1,256,512]{2,1,0:T(8,128)(2,1)}, u32[]{:S(2)}) copy-start(bf16[1,256,512]{2,1,0:T(8,128)(2,1)} %copy-done.3) | copy-start | bytes 786436
  38.2 29.9 %collective-permute-start.5 = (bf16[2,256,512]{2,1,0:T(8,128)(2,1)}, bf16[2,256,512]{2,1,0:T(8,128)(2,1)S(1)}, u32[]{:S(2)}, u32[]{:S(2)}) collective-permute-start(bf16[2,256,512]{2,1,0:T(8,128)(2,1)} %pad_maximum_fusion), channel_id=1, source_target_pairs={{8,0},{12,4},{16,8},{20,12},{24,16},{28,20},{9,1},{13,5},{17,9},{2... | collective-permute-start | bytes 1572872 | tf_op jit(solution)/shard_map/ppermute | solution.py:18
  53.4 29.4 %collective-permute-start.6 = (bf16[2,256,512]{2,1,0:T(8,128)(2,1)}, bf16[2,256,512]{2,1,0:T(8,128)(2,1)S(1)}, u32[]{:S(2)}, u32[]{:S(2)}) collective-permute-start(bf16[2,256,512]{2,1,0:T(8,128)(2,1)} %pad_maximum_fusion), channel_id=1, source_target_pairs={{12,0},{16,4},{20,8},{24,12},{28,16},{13,1},{17,5},{21,9},{25,13},... | collective-permute-start | bytes 1572872 | tf_op jit(solution)/shard_map/ppermute | solution.py:18
  63.4 46.3 %collective-permute-start.7 = (bf16[2,256,512]{2,1,0:T(8,128)(2,1)}, bf16[2,256,512]{2,1,0:T(8,128)(2,1)S(1)}, u32[]{:S(2)}, u32[]{:S(2)}) collective-permute-start(bf16[2,256,512]{2,1,0:T(8,128)(2,1)} %pad_maximum_fusion), channel_id=1, source_target_pairs={{16,0},{20,4},{24,8},{28,12},{17,1},{21,5},{25,9},{29,13},{18,2},{... | collective-permute-start | bytes 1572872 | tf_op jit(solution)/shard_map/ppermute | solution.py:18
  116.5 5.3 %copy-start.11 = (bf16[32,4,8,128]{3,2,1,0:T(8,128)(2,1)S(1)}, bf16[32,4,8,128]{3,2,1,0:T(8,128)(2,1)}, u32[]{:S(2)}) copy-start(bf16[32,4,8,128]{3,2,1,0:T(8,128)(2,1)} %fusion.16) | copy-start | bytes 786436
  136.8 2.7 copy-start.6
  136.8 3.0 %copy-start.8 = (f32[1,16]{1,0:T(1,128)S(1)}, f32[1,16]{1,0:T(1,128)}, u32[]{:S(2)}) copy-start(f32[1,16]{1,0:T(1,128)} %param.21) | copy-start | bytes 196
  138.8 50.9 %copy-start.5 = (f32[2048]{0:T(1024)S(1)}, f32[2048]{0:T(1024)}, u32[]{:S(2)}) copy-start(f32[2048]{0:T(1024)} %param.17) | copy-start | bytes 24580
  138.9 52.3 %all-gather.2.cloned.1.call-start = ((), (), s32[]{:S(2)}) async-start(), calls=%async_computation.1 | async-start | bytes 1179648 | tf_op jit(solution)/shard_map/all_gather | solution.py:97
  187.7 2.2 copy-start.2
  233.3 42.2 %copy-start.7 = (f32[16]{0:T(128)}, f32[16]{0:T(128)S(1)}, u32[]{:S(2)}) copy-start(f32[16]{0:T(128)S(1)} %get-tuple-element.7) | copy-start | bytes 196
Sparse Core Ops, SparseCore 0:
  139.0 48.6 all-reduce.16
Sparse Core Ops, SparseCore 1:
  141.7 37.6 all-gather.1
where the time goes:
time: 286 us; the launch traced here: 284 us
  waiting for transfers between devices  107 us (37%)
  blocking collectives  74.6 us (26%)
  matrix products  25.6 us (9%)
  starting transfers between devices  22.7 us (8%)
  between operations  19.7 us (7%)
  local copies, waits for them, and re-layouts  19.3 us (7%)
  other arithmetic  15.3 us (5%)
    ppermute x8, waiting for transfers between devices, shifted_2(): return lax.ppermute(x, axis, pairs)  62 us
    psum x1, waiting for transfers between devices, per_device(): attn_sum = lax.psum(partial_value, 'pb')  44.5 us
    pmax x1, blocking collectives, per_device(): all_maxima = lax.pmax(part_max, 'seq')  37.5 us
    psum x1, blocking collectives, per_device(): distill_loss = lax.psum(jnp.sum(kl_terms), ('seq', 'pb')) / query_count_all  37.1 us
    ppermute x8, starting transfers between devices, shifted_2(): return lax.ppermute(x, axis, pairs)  22.4 us
    sub x1, matrix products, per_device(): exp_terms = jnp.exp(logits - row_max)  8.77 us
    unnamed x31, local copies, waits for them, and re-layouts  6.33 us
    dot_general x1, matrix products, per_device(): jnp.einsum('hqk,khd->qhd', weights, v_heads, preferred_element_type=jnp.f...  6.15 us
  transfers between devices with their start and end apart: 10, of which 5 were waited for; matrix products, arithmetic and copies ran while one was open for 6% of the time, Pallas kernels for 0%

commit v1 on v0

--- a/solution.py
+++ b/solution.py
@@ -1,9 +1,14 @@
+import functools
+
 import jax
 import jax.numpy as jnp
 from jax import lax
+from jax.experimental import pallas as pl
+from jax.experimental.pallas import tpu as pltpu
 from jax.sharding import PartitionSpec as P
 
 HD = 128
+HEADS = 16
 WIN = 2048
 LQ = 32
 
@@ -128,6 +133,386 @@
     return (embedded, scores, score_gradient, distill_loss)
 
 
+MESH = pl.DeviceIdType.MESH
+NEG = float("-inf")
+
+
+def fused_kernel(
+    seq_count,
+    pb_count,
+    lengths_ref,
+    groups_ref,
+    tokens_ref,
+    gain_attn_ref,
+    gain_embed_ref,
+    queries_ref,
+    teacher_ref,
+    wk_hbm,
+    wv_hbm,
+    wq_hbm,
+    wo_hbm,
+    emb_hbm,
+    scores_ref,
+    grad_ref,
+    loss_ref,
+    wk,
+    wv,
+    wq,
+    wo,
+    kv_send,
+    q_send,
+    kv,
+    q_in,
+    m_send,
+    m_in,
+    query_all,
+    a_send,
+    a_in,
+    own_sum,
+    b_send,
+    b_in,
+    emb,
+    sim,
+    gmax,
+    kl_seq,
+    kl_pb,
+    w_sem,
+    out_sem,
+    send,
+    recv,
+):
+    me = lax.axis_index("seq")
+    pb = lax.axis_index("pb")
+    planes = seq_count // 2
+    z, y = me // 2, lax.rem(me, 2)
+    core = lax.rem(pb, 2)
+    core_mate = pb + 1 - 2 * core
+    x_mate = lax.rem(pb + 2, pb_count)
+    y_mate = me + 1 - 2 * y
+    rows = tokens_ref.shape[0]
+    half = rows // 2
+    chunk = half // 2
+    own_rows = pl.multiple_of(core * half, half)
+    mate_rows = pl.multiple_of((1 - core) * half, half)
+    groups = groups_ref.shape[0]
+
+    QZ, QY, KZ, KY, TQ = 0, planes, 2 * planes, 3 * planes, 4 * planes
+    MX, CA, CB, CD = 5 * planes, 6 * planes, 6 * planes + 1, 6 * planes + 3
+    GM = 6 * planes + 5
+    LS, LP = GM + seq_count, GM + 2 * seq_count
+
+    def remote(src, dst, out_place, in_place, where):
+        return pltpu.make_async_remote_copy(
+            src_ref=src,
+            dst_ref=dst,
+            send_sem=send.at[out_place],
+            recv_sem=recv.at[in_place],
+            device_id=where,
+            device_id_type=MESH,
+        )
+
+    loads = [
+        pltpu.make_async_copy(src, dst, w_sem.at[i])
+        for i, (src, dst) in enumerate(((wk_hbm, wk), (wv_hbm, wv), (wq_hbm, wq), (wo_hbm, wo)))
+    ]
+    for load in loads:
+        load.start()
+
+    barrier = pltpu.get_barrier_semaphore()
+    for d in range(1, seq_count):
+        pl.semaphore_signal(
+            barrier,
+            inc=1,
+            device_id={"seq": lax.rem(me + d, seq_count)},
+            device_id_type=MESH,
+        )
+    for d in range(1, pb_count):
+        pl.semaphore_signal(
+            barrier,
+            inc=1,
+            device_id={"pb": lax.rem(pb + d, pb_count)},
+            device_id_type=MESH,
+        )
+    query_all[me] = queries_ref[0]
+    residual = tokens_ref[...].astype(jnp.float32)
+    normed = rms_scale(residual, gain_attn_ref[...]).astype(jnp.bfloat16)
+    pl.semaphore_wait(barrier, seq_count + pb_count - 2)
+
+    def along(d):
+        return lax.rem(z + d, planes)
+
+    sent = []
+
+    def go(copy):
+        copy.start()
+        sent.append(copy)
+
+    for d in range(1, planes):
+        other = along(d)
+        go(remote(query_all.at[me], query_all.at[me], QZ + other, QZ + z, {"seq": 2 * other + y}))
+
+    loads[0].wait()
+    k_all = jnp.dot(normed, wk[...], preferred_element_type=jnp.float32).astype(jnp.bfloat16)
+    for h in range(planes):
+        kv_send[h, 0] = k_all[:, h * HD : (h + 1) * HD]
+    loads[1].wait()
+    v_all = jnp.dot(normed, wv[...], preferred_element_type=jnp.float32).astype(jnp.bfloat16)
+    for h in range(planes):
+        kv_send[h, 1] = v_all[:, h * HD : (h + 1) * HD]
+    for d in range(1, planes):
+        other = along(d)
+        go(remote(kv_send.at[other], kv.at[me], KZ + other, KZ + z, {"seq": 2 * other + y}))
+    kv[me] = kv_send[z]
+    go(remote(kv.at[me], kv.at[me], KY + z, KY + z, {"seq": y_mate}))
+    loads[2].wait()
+    q_all = jnp.dot(normed, wq[...], preferred_element_type=jnp.float32).astype(jnp.bfloat16)
+    for h in range(planes):
+        q_send[h] = q_all[:, h * HD : (h + 1) * HD]
+    for d in range(1, planes):
+        other = along(d)
+        go(remote(q_send.at[other], q_in.at[z], TQ + other, TQ + z, {"seq": 2 * other + y}))
+    q_in[z] = q_send[z]
+
+    for d in range(1, planes):
+        source = along(planes - d)
+        slot = 2 * source + y
+        remote(kv.at[slot], kv.at[slot], KZ + source, KZ + source, {"seq": slot}).wait_recv()
+        go(remote(kv.at[slot], kv.at[slot], KY + source, KY + source, {"seq": y_mate}))
+    go(remote(query_all.at[me], query_all.at[me], QY + z, QY + z, {"seq": y_mate}))
+    for d in range(1, planes):
+        source = along(planes - d)
+        slot = 2 * source + y
+        remote(query_all.at[slot], query_all.at[slot], QZ + source, QZ + source, {"seq": slot}).wait_recv()
+        go(remote(query_all.at[slot], query_all.at[slot], QY + source, QY + source, {"seq": y_mate}))
+    for d in range(planes):
+        source = along(planes - d)
+        slot = 2 * source + 1 - y
+        remote(kv.at[slot], kv.at[slot], KY + source, KY + source, {"seq": y_mate}).wait_recv()
+
+    span = rows * seq_count
+    gap = lax.broadcasted_iota(jnp.int32, (rows, span), 0) - lax.broadcasted_iota(
+        jnp.int32, (rows, span), 1
+    )
+
+    def attend(source):
+        base = (2 * source + y) * rows
+        keys = kv[:, 0].reshape(span, HD)
+        values = kv[:, 1].reshape(span, HD)
+        logits = lax.dot_general(
+            q_in[source], keys, (((1,), (1,)), ((), ())), preferred_element_type=jnp.float32
+        )
+        logits = jnp.where(jnp.abs(gap + base) <= WIN // 2, logits, NEG)
+        row_max = jnp.max(logits, axis=-1, keepdims=True)
+        terms = jnp.exp((logits - row_max) * HD ** (-0.5))
+        total = jnp.sum(terms, axis=-1, keepdims=True)
+        out = jnp.dot(terms.astype(jnp.bfloat16), values, preferred_element_type=jnp.float32)
+        return (out / total).astype(jnp.bfloat16)
+
+    def block(d, carry):
+        source = lax.rem(z + d, planes)
+        slot = 2 * source + y
+        remote(q_in.at[source], q_in.at[source], TQ + source, TQ + source, {"seq": slot}).wait_recv()
+        m_send[source] = attend(source)
+        remote(m_send.at[source], m_in.at[z], MX + source, MX + z, {"seq": slot}).start()
+        return carry
+
+    lax.fori_loop(1, planes, block, 0)
+    m_in[z] = attend(z)
+    for d in range(1, planes):
+        source = along(planes - d)
+        remote(m_in.at[source], m_in.at[source], MX + source, MX + source, {"seq": 2 * source + y}).wait_recv()
+
+    loads[3].wait()
+
+    def project(first):
+        mixed = jnp.concatenate([m_in[h, pl.ds(first, half), :] for h in range(planes)], axis=1)
+        return jnp.dot(mixed, wo[...], preferred_element_type=jnp.float32)
+
+    a_send[...] = project(mate_rows).astype(jnp.bfloat16)
+    copy_a = remote(a_send, a_in, CA, CA, {"pb": core_mate})
+    go(copy_a)
+    own_sum[...] = project(own_rows)
+    copy_a.wait_recv()
+    copies_b = []
+    for i in range(2):
+        part = slice(i * chunk, (i + 1) * chunk)
+        b_send[i] = (own_sum[part] + a_in[part].astype(jnp.float32)).astype(jnp.bfloat16)
+        copy_b = remote(b_send.at[i], b_in.at[i], CB + i, CB + i, {"pb": x_mate})
+        go(copy_b)
+        copies_b.append(copy_b)
+    for d in range(planes):
+        source = along(planes - d)
+        slot = 2 * source + 1 - y
+        remote(query_all.at[slot], query_all.at[slot], QY + source, QY + source, {"seq": y_mate}).wait_recv()
+    for i in range(2):
+        here = pl.ds(pl.multiple_of(own_rows + i * chunk, chunk), chunk)
+        copies_b[i].wait_recv()
+        attn = b_send[i].astype(jnp.float32) + b_in[i].astype(jnp.float32)
+        total = tokens_ref[here, :].astype(jnp.float32) + attn
+        emb[here, :] = rms_scale(total, gain_embed_ref[...]).astype(jnp.bfloat16)
+        go(remote(emb.at[here, :], emb.at[here, :], CD + i, CD + i, {"pb": core_mate}))
+
+    q_rows = query_all[...].reshape(query_all.shape[0] * query_all.shape[1], query_all.shape[2])
+
+    def compare(first):
+        sim[pl.ds(first, half), :] = lax.dot_general(
+            emb[pl.ds(first, half), :], q_rows, (((1,), (1,)), ((), ())), preferred_element_type=jnp.float32
+        )
+
+    compare(own_rows)
+    for i in range(2):
+        there = pl.ds(pl.multiple_of(mate_rows + i * chunk, chunk), chunk)
+        remote(emb.at[there, :], emb.at[there, :], CD + i, CD + i, {"pb": core_mate}).wait_recv()
+    store = pltpu.make_async_copy(emb, emb_hbm, out_sem)
+    store.start()
+    compare(mate_rows)
+
+    similar = sim[...]
+    position = lax.broadcasted_iota(jnp.int32, similar.shape, 0) + me * rows
+    begin = jnp.int32(0)
+    for c in range(groups):
+        end = begin + groups_ref[c]
+        inside = (position >= begin) & (position < end)
+        gmax[me, c : c + 1] = jnp.max(jnp.where(inside, similar, NEG), axis=0, keepdims=True)
+        begin = end
+    for d in range(1, seq_count):
+        other = lax.rem(me + d, seq_count)
+        go(remote(gmax.at[me], gmax.at[me], GM + other, GM + me, {"seq": other}))
+    for d in range(1, seq_count):
+        other = lax.rem(me + d, seq_count)
+        remote(gmax.at[other], gmax.at[other], GM + other, GM + other, {"seq": other}).wait_recv()
+    token_max = jnp.max(gmax[...], axis=0)
+    slot_of = lax.broadcasted_iota(jnp.int32, token_max.shape, 1) - me * LQ
+    length = lengths_ref[0]
+    live = (slot_of >= 0) & (slot_of < length)
+    column = jnp.sum(jnp.where(live, token_max, 0.0), axis=1, keepdims=True)
+    square = (groups, groups)
+    diagonal = lax.broadcasted_iota(jnp.int32, square, 0) == lax.broadcasted_iota(jnp.int32, square, 1)
+    row = jnp.sum(jnp.where(diagonal, column, 0.0), axis=0, keepdims=True)
+    scores = row / length.astype(jnp.float32)
+    scores_ref[...] = scores
+
+    def log_softmax(values):
+        values = values / SOFTMAX_TEMP
+        values = values - jnp.max(values, axis=-1, keepdims=True)
+        return values - jnp.log(jnp.sum(jnp.exp(values), axis=-1, keepdims=True))
+
+    log_s = log_softmax(scores)
+    log_t = log_softmax(teacher_ref[...])
+    prob = jnp.exp(log_t)
+    amount = seq_count * pb_count
+    grad_ref[...] = (jnp.exp(log_s) - prob) / (SOFTMAX_TEMP * amount)
+    kl = jnp.sum(prob * (log_t - log_s), axis=-1, keepdims=True)
+    kl_seq[me] = jnp.broadcast_to(kl, kl_seq.shape[1:])
+    for d in range(1, seq_count):
+        other = lax.rem(me + d, seq_count)
+        go(remote(kl_seq.at[me], kl_seq.at[me], LS + other, LS + me, {"seq": other}))
+    for d in range(1, seq_count):
+        other = lax.rem(me + d, seq_count)
+        remote(kl_seq.at[other], kl_seq.at[other], LS + other, LS + other, {"seq": other}).wait_recv()
+    kl_pb[pb] = jnp.sum(kl_seq[...], axis=0)
+    for d in range(1, pb_count):
+        other = lax.rem(pb + d, pb_count)
+        go(remote(kl_pb.at[pb], kl_pb.at[pb], LP + other, LP + pb, {"pb": other}))
+    for d in range(1, pb_count):
+        other = lax.rem(pb + d, pb_count)
+        remote(kl_pb.at[other], kl_pb.at[other], LP + other, LP + other, {"pb": other}).wait_recv()
+    loss_ref[...] = jnp.sum(kl_pb[...], axis=0)[:1, :1] / amount
+
+    for copy in sent:
+        copy.wait_send()
+    for d in range(1, planes):
+        other = along(d)
+        remote(m_send.at[other], m_in.at[z], MX + other, MX + z, {"seq": 2 * other + y}).wait_send()
+    store.wait()
+
+
+def fused(
+    tokens,
+    w_query,
+    w_key,
+    w_value,
+    w_out,
+    gain_attn,
+    gain_embed,
+    queries,
+    query_lengths,
+    group_lengths,
+    teacher,
+):
+    seq_count, pb_count = lax.axis_size("seq"), lax.axis_size("pb")
+    rows, width = tokens.shape
+    head_width = w_query.shape[1]
+    planes = seq_count // 2
+    groups = group_lengths.shape[0]
+    slots = queries.shape[0] * seq_count * LQ
+    half = rows // 2
+    bf, f32 = jnp.bfloat16, jnp.float32
+    vmem, smem = pl.BlockSpec(memory_space=pltpu.VMEM), pl.BlockSpec(memory_space=pltpu.SMEM)
+    hbm = pl.BlockSpec(memory_space=pl.ANY)
+    copies = 6 * planes + 5 + 2 * seq_count + pb_count
+    embedded, scores, grad, loss = pl.pallas_call(
+        functools.partial(fused_kernel, seq_count, pb_count),
+        out_shape=(
+            jax.ShapeDtypeStruct((rows, width), bf),
+            jax.ShapeDtypeStruct((1, groups), f32),
+            jax.ShapeDtypeStruct((1, groups), f32),
+            jax.ShapeDtypeStruct((1, 1), f32),
+        ),
+        in_specs=[smem, smem] + [vmem] * 5 + [hbm] * 4,
+        out_specs=(hbm, vmem, vmem, vmem),
+        scratch_shapes=[
+            pltpu.VMEM((width, head_width), bf),
+            pltpu.VMEM((width, head_width), bf),
+            pltpu.VMEM((width, head_width), bf),
+            pltpu.VMEM((head_width, width), bf),
+            pltpu.VMEM((planes, 2, rows, HD), bf),
+            pltpu.VMEM((planes, rows, HD), bf),
+            pltpu.VMEM((seq_count, 2, rows, HD), bf),
+            pltpu.VMEM((planes, rows, HD), bf),
+            pltpu.VMEM((planes, rows, HD), bf),
+            pltpu.VMEM((planes, rows, HD), bf),
+            pltpu.VMEM((seq_count, LQ, width), bf),
+            pltpu.VMEM((half, width), bf),
+            pltpu.VMEM((half, width), bf),
+            pltpu.VMEM((half, width), f32),
+            pltpu.VMEM((2, half // 2, width), bf),
+            pltpu.VMEM((2, half // 2, width), bf),
+            pltpu.VMEM((rows, width), bf),
+            pltpu.VMEM((rows, slots), f32),
+            pltpu.VMEM((seq_count, groups, slots), f32),
+            pltpu.VMEM((seq_count, 8, 128), f32),
+            pltpu.VMEM((pb_count, 8, 128), f32),
+            pltpu.SemaphoreType.DMA((4,)),
+            pltpu.SemaphoreType.DMA,
+            pltpu.SemaphoreType.DMA((copies,)),
+            pltpu.SemaphoreType.DMA((copies,)),
+        ],
+        compiler_params=pltpu.CompilerParams(
+            collective_id=0, has_side_effects=True, vmem_limit_bytes=56 * 1024 * 1024
+        ),
+    )(
+        query_lengths,
+        group_lengths,
+        tokens,
+        gain_attn.reshape(1, width),
+        gain_embed.reshape(1, width),
+        queries,
+        teacher,
+        w_key,
+        w_value,
+        w_query,
+        w_out,
+    )
+    return embedded, scores, grad, loss.reshape(())
+
+
+def run(*args):
+    planes = args[1].shape[1] // HD
+    fits = lax.axis_size("seq") == 2 * planes and lax.axis_size("pb") == 4 and args[7].shape[0] == 1
+    return fused(*args) if fits else per_device(*args)
+
+
 def solution(mesh):
     placed = (
         P("seq", None),
@@ -143,7 +528,7 @@
         P(("seq", "pb"), None),
     )
     return jax.shard_map(
-        per_device,
+        run,
         mesh=mesh,
         in_specs=placed,
         out_specs=(P("seq", None), P(("seq", "pb"), None), P(("seq", "pb"), None), P()),

time: 286 us -> 87.5 us (0.31)
  waiting for transfers between devices: 107 us -> 0 us
  Pallas kernels: 0 us -> 80.9 us
  blocking collectives: 74.6 us -> 0 us
  matrix products: 25.6 us -> 0 us
  starting transfers between devices: 22.7 us -> 0 us
  between operations: 19.7 us -> 3.12 us
  local copies, waits for them, and re-layouts: 19.3 us -> 3.33 us
  other arithmetic: 15.3 us -> 0 us
    pallas_call x0 -> x1, Pallas kernels: none -> 80.9 us  [fused(): pl.pallas_call(functools.partial(fused_kernel, seq_count, pb_count), out_...]
    ppermute x8 -> x0, waiting for transfers between devices: 62 us -> none  [shifted_2(): return lax.ppermute(x, axis, pairs)]
    psum x1 -> x0, waiting for transfers between devices: 44.5 us -> none  [per_device(): attn_sum = lax.psum(partial_value, 'pb')]
    pmax x1 -> x0, blocking collectives: 37.5 us -> none  [per_device(): all_maxima = lax.pmax(part_max, 'seq')]
    psum x1 -> x0, blocking collectives: 37.1 us -> none  [per_device(): distill_loss = lax.psum(jnp.sum(kl_terms), ('seq', 'pb')) / query_count_all]
    ppermute x8 -> x0, starting transfers between devices: 22.4 us -> none  [shifted_2(): return lax.ppermute(x, axis, pairs)]
    dot_general x6 -> x0, matrix products: 16.8 us -> none  [the longest x1 6.15 us: per_device(): jnp.einsum('hqk,khd->qhd', weights, v_heads, preferred_element_type=jnp.f...]
    another operation x2 -> x0, local copies, waits for them, and re-layouts: 9.65 us -> none  [the longest x1 5.31 us: per_device(): k_heads = window[0].reshape(span_rows, heads_here, HD)]
  transfers between devices with their start and end apart: 10 -> 0, of which waited for: 5 -> 0; matrix products, arithmetic and copies ran while one was open for 6% -> 0% of each run, Pallas kernels for 0% -> 0%
where the time goes in v1:
time: 87.5 us; the launch traced here: 87.4 us
  Pallas kernels  80.9 us (92%)
  local copies, waits for them, and re-layouts  3.33 us (4%)
  between operations  3.12 us (4%)
    pallas_call x1, Pallas kernels, fused(): pl.pallas_call(functools.partial(fused_kernel, seq_count, pb_count), out_...  80.9 us
    unnamed x7, local copies, waits for them, and re-layouts  3.33 us

profile of v1, /device:TPU:0, one launch (start us, length us, event | category | flops | bytes accessed | tf_op | source)
XLA Modules:
  0.0 87.4 jit_solution(3967116068145597875)
XLA Ops:
  1.3 80.9 %shard_map.138 = (bf16[256,2048]{1,0:T(8,128)(2,1)}, f32[1,16]{1,0:T(1,128)}, f32[1,16]{1,0:T(1,128)}, f32[1,1]{1,0:T(1,128)}) custom-call(s32[1]{0:T(128)S(6)} %copy.19.lengths_ref, s32[16]{0:T(128)} %groups_ref.1, bf16[256,2048]{1,0:T(8,128)(2,1)} %tokens_ref.1, f32[1,2048]{1,0:T(1,128)} %bitcast.3, f32[1,2048]{1,0:T(1,128)} %bitcast.4, ...), custom_call_target="tpu_custom_call" | custom-call | tf_op jit(solution)/shard_map/pallas_call | solution.py:454
  82.2 0.0 copy-start.1
  82.2 0.0 copy-start
  82.2 2.3 %copy.20 = bf16[256,2048]{1,0:T(8,128)(2,1)} copy(bf16[256,2048]{1,0:T(8,128)(2,1)} %get-tuple-element.16) | data formatting | bytes 2097152
  84.5 0.0 copy-done.1
  84.5 0.5 copy.21
  85.0 0.0 copy-done
  85.0 0.5 copy.22
Async XLA Ops:
  82.2 2.3 %copy-start.1 = (f32[1,16]{1,0:T(1,128)S(1)}, f32[1,16]{1,0:T(1,128)}, u32[]{:S(2)}) copy-start(f32[1,16]{1,0:T(1,128)} %get-tuple-element.17) | copy-start | bytes 196
  82.2 2.8 %copy-start = (f32[1,16]{1,0:T(1,128)S(1)}, f32[1,16]{1,0:T(1,128)}, u32[]{:S(2)}) copy-start(f32[1,16]{1,0:T(1,128)} %get-tuple-element.18) | copy-start | bytes 196

commit v2 on v1

--- a/solution.py
+++ b/solution.py
@@ -169,8 +169,6 @@
     a_send,
     a_in,
     own_sum,
-    b_send,
-    b_in,
     emb,
     sim,
     gmax,
@@ -185,7 +183,7 @@
     pb = lax.axis_index("pb")
     planes = seq_count // 2
     z, y = me // 2, lax.rem(me, 2)
-    core = lax.rem(pb, 2)
+    core, x = lax.rem(pb, 2), pb // 2
     core_mate = pb + 1 - 2 * core
     x_mate = lax.rem(pb + 2, pb_count)
     y_mate = me + 1 - 2 * y
@@ -196,9 +194,9 @@
     mate_rows = pl.multiple_of((1 - core) * half, half)
     groups = groups_ref.shape[0]
 
-    QZ, QY, KZ, KY, TQ = 0, planes, 2 * planes, 3 * planes, 4 * planes
-    MX, CA, CB, CD = 5 * planes, 6 * planes, 6 * planes + 1, 6 * planes + 3
-    GM = 6 * planes + 5
+    QU, QD, QY, KZ, KY, TQ, MX, XX = (i * planes for i in range(8))
+    CA, WX, CD = 8 * planes, 8 * planes + 1, 8 * planes + 2
+    GM = 8 * planes + 4
     LS, LP = GM + seq_count, GM + 2 * seq_count
 
     def remote(src, dst, out_place, in_place, where):
@@ -213,7 +211,7 @@
 
     loads = [
         pltpu.make_async_copy(src, dst, w_sem.at[i])
-        for i, (src, dst) in enumerate(((wk_hbm, wk), (wv_hbm, wv), (wq_hbm, wq), (wo_hbm, wo)))
+        for i, (src, dst) in enumerate(((wk_hbm, wk), (wv_hbm, wv), (wq_hbm, wq), (wo_hbm, wo.at[x])))
     ]
     for load in loads:
         load.start()
@@ -247,9 +245,38 @@
         copy.start()
         sent.append(copy)
 
-    for d in range(1, planes):
-        other = along(d)
-        go(remote(query_all.at[me], query_all.at[me], QZ + other, QZ + z, {"seq": 2 * other + y}))
+    go(remote(wo_hbm, wo.at[x], WX, WX, {"pb": x_mate}))
+
+    def hop(far):
+        upward, downward = 2 * (z - far) + y, 2 * (z + far) + y
+        up = remote(query_all.at[upward], query_all.at[upward], QU + z - far, QU + z - far, {"seq": me + 2})
+        down = remote(query_all.at[downward], query_all.at[downward], QD + z + far, QD + z + far, {"seq": me - 2})
+        return ((z >= far) & (z < planes - 1), up), ((z + far < planes) & (z > 0), down)
+
+    def hop_in(far):
+        for sign in (-1, 1):
+            source = z + sign * far
+            slot = 2 * source + y
+
+            @pl.when((source >= 0) & (source < planes))
+            def _():
+                block = query_all.at[slot]
+                place = (QU if sign < 0 else QD) + source
+                remote(block, block, place, place, {"seq": me + 2 * sign}).wait_recv()
+
+    def hop_out(far):
+        for valid, copy in hop(far):
+            pl.when(valid)(copy.start)
+        for sign in (-1, 1) if far else (1,):
+            source = z + sign * far
+            slot = 2 * source + y
+
+            @pl.when((source >= 0) & (source < planes))
+            def _():
+                block = query_all.at[slot]
+                remote(block, block, QY + source, QY + source, {"seq": y_mate}).start()
+
+    hop_out(0)
 
     loads[0].wait()
     k_all = jnp.dot(normed, wk[...], preferred_element_type=jnp.float32).astype(jnp.bfloat16)
@@ -268,9 +295,6 @@
     q_all = jnp.dot(normed, wq[...], preferred_element_type=jnp.float32).astype(jnp.bfloat16)
     for h in range(planes):
         q_send[h] = q_all[:, h * HD : (h + 1) * HD]
-    for d in range(1, planes):
-        other = along(d)
-        go(remote(q_send.at[other], q_in.at[z], TQ + other, TQ + z, {"seq": 2 * other + y}))
     q_in[z] = q_send[z]
 
     for d in range(1, planes):
@@ -278,12 +302,9 @@
         slot = 2 * source + y
         remote(kv.at[slot], kv.at[slot], KZ + source, KZ + source, {"seq": slot}).wait_recv()
         go(remote(kv.at[slot], kv.at[slot], KY + source, KY + source, {"seq": y_mate}))
-    go(remote(query_all.at[me], query_all.at[me], QY + z, QY + z, {"seq": y_mate}))
     for d in range(1, planes):
-        source = along(planes - d)
-        slot = 2 * source + y
-        remote(query_all.at[slot], query_all.at[slot], QZ + source, QZ + source, {"seq": slot}).wait_recv()
-        go(remote(query_all.at[slot], query_all.at[slot], QY + source, QY + source, {"seq": y_mate}))
+        other = along(d)
+        go(remote(q_send.at[other], q_in.at[z], TQ + other, TQ + z, {"seq": 2 * other + y}))
     for d in range(planes):
         source = along(planes - d)
         slot = 2 * source + 1 - y
@@ -308,46 +329,55 @@
         out = jnp.dot(terms.astype(jnp.bfloat16), values, preferred_element_type=jnp.float32)
         return (out / total).astype(jnp.bfloat16)
 
-    def block(d, carry):
-        source = lax.rem(z + d, planes)
+    def over(h):
+        return remote(m_in.at[x, h], m_in.at[x, h], XX + h, XX + h, {"pb": x_mate})
+
+    hop_in(1)
+    hop_out(1)
+    m_in[x, z] = attend(z)
+    go(over(z))
+    for d in range(1, planes):
+        source = along(d)
         slot = 2 * source + y
         remote(q_in.at[source], q_in.at[source], TQ + source, TQ + source, {"seq": slot}).wait_recv()
         m_send[source] = attend(source)
-        remote(m_send.at[source], m_in.at[z], MX + source, MX + z, {"seq": slot}).start()
-        return carry
-
-    lax.fori_loop(1, planes, block, 0)
-    m_in[z] = attend(z)
+        go(remote(m_send.at[source], m_in.at[x, z], MX + source, MX + z, {"seq": slot}))
+        if d + 1 < planes:
+            hop_in(d + 1)
+            hop_out(d + 1)
     for d in range(1, planes):
         source = along(planes - d)
-        remote(m_in.at[source], m_in.at[source], MX + source, MX + source, {"seq": 2 * source + y}).wait_recv()
+        block = m_in.at[x, source]
+        remote(block, block, MX + source, MX + source, {"seq": 2 * source + y}).wait_recv()
+        go(over(source))
 
     loads[3].wait()
 
+    remote(wo.at[1 - x], wo.at[1 - x], WX, WX, {"pb": x_mate}).wait_recv()
+    for h in range(planes):
+        block = m_in.at[1 - x, h]
+        remote(block, block, XX + h, XX + h, {"pb": x_mate}).wait_recv()
+
     def project(first):
-        mixed = jnp.concatenate([m_in[h, pl.ds(first, half), :] for h in range(planes)], axis=1)
-        return jnp.dot(mixed, wo[...], preferred_element_type=jnp.float32)
+        mixed = jnp.concatenate(
+            [m_in[i, h, pl.ds(first, half), :] for i in range(2) for h in range(planes)], axis=1
+        )
+        weight = wo[...].reshape(2 * wo.shape[1], wo.shape[2])
+        return jnp.dot(mixed, weight, preferred_element_type=jnp.float32)
 
     a_send[...] = project(mate_rows).astype(jnp.bfloat16)
     copy_a = remote(a_send, a_in, CA, CA, {"pb": core_mate})
     go(copy_a)
     own_sum[...] = project(own_rows)
     copy_a.wait_recv()
-    copies_b = []
-    for i in range(2):
-        part = slice(i * chunk, (i + 1) * chunk)
-        b_send[i] = (own_sum[part] + a_in[part].astype(jnp.float32)).astype(jnp.bfloat16)
-        copy_b = remote(b_send.at[i], b_in.at[i], CB + i, CB + i, {"pb": x_mate})
-        go(copy_b)
-        copies_b.append(copy_b)
     for d in range(planes):
         source = along(planes - d)
         slot = 2 * source + 1 - y
         remote(query_all.at[slot], query_all.at[slot], QY + source, QY + source, {"seq": y_mate}).wait_recv()
     for i in range(2):
         here = pl.ds(pl.multiple_of(own_rows + i * chunk, chunk), chunk)
-        copies_b[i].wait_recv()
-        attn = b_send[i].astype(jnp.float32) + b_in[i].astype(jnp.float32)
+        part = slice(i * chunk, (i + 1) * chunk)
+        attn = own_sum[part] + a_in[part].astype(jnp.float32)
         total = tokens_ref[here, :].astype(jnp.float32) + attn
         emb[here, :] = rms_scale(total, gain_embed_ref[...]).astype(jnp.bfloat16)
         go(remote(emb.at[here, :], emb.at[here, :], CD + i, CD + i, {"pb": core_mate}))
@@ -421,9 +451,12 @@
 
     for copy in sent:
         copy.wait_send()
-    for d in range(1, planes):
-        other = along(d)
-        remote(m_send.at[other], m_in.at[z], MX + other, MX + z, {"seq": 2 * other + y}).wait_send()
+    for far in range(planes):
+        for valid, copy in hop(far):
+            pl.when(valid)(copy.wait_send)
+    for source in range(planes):
+        block = query_all.at[2 * source + y]
+        remote(block, block, QY + source, QY + source, {"seq": y_mate}).wait_send()
     store.wait()
 
 
@@ -450,7 +483,7 @@
     bf, f32 = jnp.bfloat16, jnp.float32
     vmem, smem = pl.BlockSpec(memory_space=pltpu.VMEM), pl.BlockSpec(memory_space=pltpu.SMEM)
     hbm = pl.BlockSpec(memory_space=pl.ANY)
-    copies = 6 * planes + 5 + 2 * seq_count + pb_count
+    copies = 8 * planes + 4 + 2 * seq_count + pb_count
     embedded, scores, grad, loss = pl.pallas_call(
         functools.partial(fused_kernel, seq_count, pb_count),
         out_shape=(
@@ -465,19 +498,17 @@
             pltpu.VMEM((width, head_width), bf),
             pltpu.VMEM((width, head_width), bf),
             pltpu.VMEM((width, head_width), bf),
-            pltpu.VMEM((head_width, width), bf),
+            pltpu.VMEM((2, head_width, width), bf),
             pltpu.VMEM((planes, 2, rows, HD), bf),
             pltpu.VMEM((planes, rows, HD), bf),
             pltpu.VMEM((seq_count, 2, rows, HD), bf),
             pltpu.VMEM((planes, rows, HD), bf),
             pltpu.VMEM((planes, rows, HD), bf),
-            pltpu.VMEM((planes, rows, HD), bf),
+            pltpu.VMEM((2, planes, rows, HD), bf),
             pltpu.VMEM((seq_count, LQ, width), bf),
             pltpu.VMEM((half, width), bf),
             pltpu.VMEM((half, width), bf),
             pltpu.VMEM((half, width), f32),
-            pltpu.VMEM((2, half // 2, width), bf),
-            pltpu.VMEM((2, half // 2, width), bf),
             pltpu.VMEM((rows, width), bf),
             pltpu.VMEM((rows, slots), f32),
             pltpu.VMEM((seq_count, groups, slots), f32),

time: 87.5 us -> 85.4 us (0.976)
  Pallas kernels: 80.9 us -> 78.8 us
    pallas_call x1, Pallas kernels: 80.9 us -> 78.8 us  [fused(): pl.pallas_call(functools.partial(fused_kernel, seq_count, pb_count), out_...]
where the time goes in v2:
time: 85.4 us; the launch traced here: 85.2 us
  Pallas kernels  78.8 us (92%)
  local copies, waits for them, and re-layouts  3.33 us (4%)
  between operations  3.12 us (4%)
    pallas_call x1, Pallas kernels, fused(): pl.pallas_call(functools.partial(fused_kernel, seq_count, pb_count), out_...  78.8 us
    unnamed x7, local copies, waits for them, and re-layouts  3.33 us

profile of v2, /device:TPU:0, one launch (start us, length us, event | category | flops | bytes accessed | tf_op | source)
XLA Modules:
  0.0 85.2 jit_solution(13246088772285250385)
XLA Ops:
  1.3 78.8 %shard_map.138 = (bf16[256,2048]{1,0:T(8,128)(2,1)}, f32[1,16]{1,0:T(1,128)}, f32[1,16]{1,0:T(1,128)}, f32[1,1]{1,0:T(1,128)}) custom-call(s32[1]{0:T(128)S(6)} %copy.19.lengths_ref, s32[16]{0:T(128)} %groups_ref.1, bf16[256,2048]{1,0:T(8,128)(2,1)} %tokens_ref.1, f32[1,2048]{1,0:T(1,128)} %bitcast.3, f32[1,2048]{1,0:T(1,128)} %bitcast.4, ...), custom_call_target="tpu_custom_call" | custom-call | tf_op jit(solution)/shard_map/pallas_call | solution.py:487
  80.1 0.0 copy-start.1
  80.1 0.0 copy-start
  80.1 2.3 %copy.20 = bf16[256,2048]{1,0:T(8,128)(2,1)} copy(bf16[256,2048]{1,0:T(8,128)(2,1)} %get-tuple-element.16) | data formatting | bytes 2097152
  82.4 0.0 copy-done.1
  82.4 0.5 copy.21
  82.9 0.0 copy-done
  82.9 0.5 copy.22
Async XLA Ops:
  80.1 2.3 %copy-start.1 = (f32[1,16]{1,0:T(1,128)S(1)}, f32[1,16]{1,0:T(1,128)}, u32[]{:S(2)}) copy-start(f32[1,16]{1,0:T(1,128)} %get-tuple-element.17) | copy-start | bytes 196
  80.1 2.8 %copy-start = (f32[1,16]{1,0:T(1,128)S(1)}, f32[1,16]{1,0:T(1,128)}, u32[]{:S(2)}) copy-start(f32[1,16]{1,0:T(1,128)} %get-tuple-element.18) | copy-start | bytes 196

commit v3 on v2

--- a/solution.py
+++ b/solution.py
@@ -151,7 +151,7 @@
     wv_hbm,
     wq_hbm,
     wo_hbm,
-    emb_hbm,
+    emb_ref,
     scores_ref,
     grad_ref,
     loss_ref,
@@ -195,8 +195,9 @@
     groups = groups_ref.shape[0]
 
     QU, QD, QY, KZ, KY, TQ, MX, XX = (i * planes for i in range(8))
-    CA, WX, CD = 8 * planes, 8 * planes + 1, 8 * planes + 2
-    GM = 8 * planes + 4
+    CA, CD, WX = 8 * planes, 8 * planes + 1, 8 * planes + 3
+    WY = WX + planes - 1
+    GM = WY + 1
     LS, LP = GM + seq_count, GM + 2 * seq_count
 
     def remote(src, dst, out_place, in_place, where):
@@ -245,7 +246,19 @@
         copy.start()
         sent.append(copy)
 
-    go(remote(wo_hbm, wo.at[x], WX, WX, {"pb": x_mate}))
+    def wanted(i):
+        return y * (planes - 1) + (1 - 2 * y) * i
+
+    def fetch(i):
+        h = wanted(i)
+        return remote(wo_hbm.at[h], wo.at[x, h], WX + i, WX + i, {"pb": x_mate})
+
+    def fetched(i):
+        block = wo.at[1 - x, wanted(i)]
+        remote(block, block, WX + i, WX + i, {"pb": x_mate}).wait_recv()
+
+    for i in range(planes - 2):
+        go(fetch(i))
 
     def hop(far):
         upward, downward = 2 * (z - far) + y, 2 * (z + far) + y
@@ -311,18 +324,18 @@
         remote(kv.at[slot], kv.at[slot], KY + source, KY + source, {"seq": y_mate}).wait_recv()
 
     span = rows * seq_count
-    gap = lax.broadcasted_iota(jnp.int32, (rows, span), 0) - lax.broadcasted_iota(
-        jnp.int32, (rows, span), 1
-    )
+    key_at = lax.broadcasted_iota(jnp.int32, (1, span), 1)
+    row_at = lax.broadcasted_iota(jnp.int32, (rows, 1), 0)
 
     def attend(source):
-        base = (2 * source + y) * rows
+        query_at = row_at + (2 * source + y) * rows
+        seen = (key_at >= query_at - WIN // 2) & (key_at <= query_at + WIN // 2)
         keys = kv[:, 0].reshape(span, HD)
         values = kv[:, 1].reshape(span, HD)
         logits = lax.dot_general(
             q_in[source], keys, (((1,), (1,)), ((), ())), preferred_element_type=jnp.float32
         )
-        logits = jnp.where(jnp.abs(gap + base) <= WIN // 2, logits, NEG)
+        logits = jnp.where(seen, logits, NEG)
         row_max = jnp.max(logits, axis=-1, keepdims=True)
         terms = jnp.exp((logits - row_max) * HD ** (-0.5))
         total = jnp.sum(terms, axis=-1, keepdims=True)
@@ -332,6 +345,10 @@
     def over(h):
         return remote(m_in.at[x, h], m_in.at[x, h], XX + h, XX + h, {"pb": x_mate})
 
+    go(fetch(planes - 2))
+    fetched(0)
+    first = wo.at[1 - x, wanted(0)]
+    go(remote(first, first, WY, WY, {"seq": y_mate}))
     hop_in(1)
     hop_out(1)
     m_in[x, z] = attend(z)
@@ -353,7 +370,10 @@
 
     loads[3].wait()
 
-    remote(wo.at[1 - x], wo.at[1 - x], WX, WX, {"pb": x_mate}).wait_recv()
+    for i in range(1, planes - 1):
+        fetched(i)
+    last = wo.at[1 - x, wanted(planes - 1)]
+    remote(last, last, WY, WY, {"seq": y_mate}).wait_recv()
     for h in range(planes):
         block = m_in.at[1 - x, h]
         remote(block, block, XX + h, XX + h, {"pb": x_mate}).wait_recv()
@@ -362,7 +382,7 @@
         mixed = jnp.concatenate(
             [m_in[i, h, pl.ds(first, half), :] for i in range(2) for h in range(planes)], axis=1
         )
-        weight = wo[...].reshape(2 * wo.shape[1], wo.shape[2])
+        weight = wo[...].reshape(2 * planes * HD, wo.shape[3])
         return jnp.dot(mixed, weight, preferred_element_type=jnp.float32)
 
     a_send[...] = project(mate_rows).astype(jnp.bfloat16)
@@ -393,7 +413,7 @@
     for i in range(2):
         there = pl.ds(pl.multiple_of(mate_rows + i * chunk, chunk), chunk)
         remote(emb.at[there, :], emb.at[there, :], CD + i, CD + i, {"pb": core_mate}).wait_recv()
-    store = pltpu.make_async_copy(emb, emb_hbm, out_sem)
+    store = pltpu.make_async_copy(emb, emb_ref, out_sem)
     store.start()
     compare(mate_rows)
 
@@ -483,22 +503,22 @@
     bf, f32 = jnp.bfloat16, jnp.float32
     vmem, smem = pl.BlockSpec(memory_space=pltpu.VMEM), pl.BlockSpec(memory_space=pltpu.SMEM)
     hbm = pl.BlockSpec(memory_space=pl.ANY)
-    copies = 8 * planes + 4 + 2 * seq_count + pb_count
+    copies = 9 * planes + 3 + 2 * seq_count + pb_count
     embedded, scores, grad, loss = pl.pallas_call(
         functools.partial(fused_kernel, seq_count, pb_count),
         out_shape=(
-            jax.ShapeDtypeStruct((rows, width), bf),
+            pltpu.VMEM((rows, width), bf),
             jax.ShapeDtypeStruct((1, groups), f32),
             jax.ShapeDtypeStruct((1, groups), f32),
             jax.ShapeDtypeStruct((1, 1), f32),
         ),
         in_specs=[smem, smem] + [vmem] * 5 + [hbm] * 4,
-        out_specs=(hbm, vmem, vmem, vmem),
+        out_specs=(vmem, vmem, vmem, vmem),
         scratch_shapes=[
             pltpu.VMEM((width, head_width), bf),
             pltpu.VMEM((width, head_width), bf),
             pltpu.VMEM((width, head_width), bf),
-            pltpu.VMEM((2, head_width, width), bf),
+            pltpu.VMEM((2, planes, HD, width), bf),
             pltpu.VMEM((planes, 2, rows, HD), bf),
             pltpu.VMEM((planes, rows, HD), bf),
             pltpu.VMEM((seq_count, 2, rows, HD), bf),
@@ -533,7 +553,7 @@
         w_key,
         w_value,
         w_query,
-        w_out,
+        w_out.reshape(planes, HD, width),
     )
     return embedded, scores, grad, loss.reshape(())
 

time: 85.4 us -> 73.1 us (0.86)
  Pallas kernels: 78.8 us -> 67.9 us
  local copies, waits for them, and re-layouts: 3.33 us -> 2 us
    pallas_call x1, Pallas kernels: 78.8 us -> 67.9 us  [fused(): pl.pallas_call(functools.partial(fused_kernel, seq_count, pb_count), out_...]
    unnamed x7, local copies, waits for them, and re-layouts: 3.33 us -> 2 us
where the time goes in v3:
time: 73.1 us; the launch traced here: 72.9 us
  Pallas kernels  67.9 us (93%)
  between operations  3.05 us (4%)
  local copies, waits for them, and re-layouts  2 us (3%)
    pallas_call x1, Pallas kernels, fused(): pl.pallas_call(functools.partial(fused_kernel, seq_count, pb_count), out_...  67.9 us
    unnamed x7, local copies, waits for them, and re-layouts  2 us

profile of v3, /device:TPU:0, one launch (start us, length us, event | category | flops | bytes accessed | tf_op | source)
XLA Modules:
  0.0 72.9 jit_solution(9394143512114360630)
XLA Ops:
  1.3 67.9 %shard_map.138 = (bf16[256,2048]{1,0:T(8,128)(2,1)S(1)}, f32[1,16]{1,0:T(1,128)}, f32[1,16]{1,0:T(1,128)}, f32[1,1]{1,0:T(1,128)}) custom-call(s32[1]{0:T(128)S(6)} %copy.20.lengths_ref, s32[16]{0:T(128)} %groups_ref.1, bf16[256,2048]{1,0:T(8,128)(2,1)} %tokens_ref.1, f32[1,2048]{1,0:T(1,128)} %bitcast.5, f32[1,2048]{1,0:T(1,128)} %bitcast.6, ...), custom_call_target="tpu_custom_call" | custom-call | tf_op jit(solution)/shard_map/pallas_call | solution.py:507
  69.2 0.0 copy-start.1
  69.2 0.0 copy-start
  69.2 1.0 %copy.19 = bf16[256,2048]{1,0:T(8,128)(2,1)} copy(bf16[256,2048]{1,0:T(8,128)(2,1)S(1)} %get-tuple-element.12) | data formatting | bytes 2097152
  70.1 0.0 copy-done.1
  70.2 0.5 copy.21
  70.7 0.0 copy-done
  70.7 0.5 copy.22
Async XLA Ops:
  69.2 1.0 %copy-start.1 = (f32[1,16]{1,0:T(1,128)S(1)}, f32[1,16]{1,0:T(1,128)}, u32[]{:S(2)}) copy-start(f32[1,16]{1,0:T(1,128)} %get-tuple-element.21) | copy-start | bytes 196
  69.2 1.5 %copy-start = (f32[1,16]{1,0:T(1,128)S(1)}, f32[1,16]{1,0:T(1,128)}, u32[]{:S(2)}) copy-start(f32[1,16]{1,0:T(1,128)} %get-tuple-element.22) | copy-start | bytes 196

commit v4 on v3

--- a/solution.py
+++ b/solution.py
@@ -1,4 +1,5 @@
 import functools
+import math
 
 import jax
 import jax.numpy as jnp
@@ -199,6 +200,7 @@
     WY = WX + planes - 1
     GM = WY + 1
     LS, LP = GM + seq_count, GM + 2 * seq_count
+    VZ = LP + pb_count
 
     def remote(src, dst, out_place, in_place, where):
         return pltpu.make_async_remote_copy(
@@ -214,7 +216,7 @@
         pltpu.make_async_copy(src, dst, w_sem.at[i])
         for i, (src, dst) in enumerate(((wk_hbm, wk), (wv_hbm, wv), (wq_hbm, wq), (wo_hbm, wo.at[x])))
     ]
-    for load in loads:
+    for load in loads[:2]:
         load.start()
 
     barrier = pltpu.get_barrier_semaphore()
@@ -236,6 +238,7 @@
     residual = tokens_ref[...].astype(jnp.float32)
     normed = rms_scale(residual, gain_attn_ref[...]).astype(jnp.bfloat16)
     pl.semaphore_wait(barrier, seq_count + pb_count - 2)
+    loads[2].start()
 
     def along(d):
         return lax.rem(z + d, planes)
@@ -295,13 +298,19 @@
     k_all = jnp.dot(normed, wk[...], preferred_element_type=jnp.float32).astype(jnp.bfloat16)
     for h in range(planes):
         kv_send[h, 0] = k_all[:, h * HD : (h + 1) * HD]
+
+    def scatter(which, place):
+        for d in range(1, planes):
+            other = along(d)
+            go(remote(kv_send.at[other, which], kv.at[me, which], place + other, place + z, {"seq": 2 * other + y}))
+
+    scatter(0, KZ)
+    loads[3].start()
     loads[1].wait()
     v_all = jnp.dot(normed, wv[...], preferred_element_type=jnp.float32).astype(jnp.bfloat16)
     for h in range(planes):
         kv_send[h, 1] = v_all[:, h * HD : (h + 1) * HD]
-    for d in range(1, planes):
-        other = along(d)
-        go(remote(kv_send.at[other], kv.at[me], KZ + other, KZ + z, {"seq": 2 * other + y}))
+    scatter(1, VZ)
     kv[me] = kv_send[z]
     go(remote(kv.at[me], kv.at[me], KY + z, KY + z, {"seq": y_mate}))
     loads[2].wait()
@@ -313,7 +322,9 @@
     for d in range(1, planes):
         source = along(planes - d)
         slot = 2 * source + y
-        remote(kv.at[slot], kv.at[slot], KZ + source, KZ + source, {"seq": slot}).wait_recv()
+        for which, place in ((0, KZ), (1, VZ)):
+            block = kv.at[slot, which]
+            remote(block, block, place + source, place + source, {"seq": slot}).wait_recv()
         go(remote(kv.at[slot], kv.at[slot], KY + source, KY + source, {"seq": y_mate}))
     for d in range(1, planes):
         other = along(d)
@@ -337,7 +348,7 @@
         )
         logits = jnp.where(seen, logits, NEG)
         row_max = jnp.max(logits, axis=-1, keepdims=True)
-        terms = jnp.exp((logits - row_max) * HD ** (-0.5))
+        terms = jnp.exp2((logits - row_max) * (HD ** (-0.5) / math.log(2.0)))
         total = jnp.sum(terms, axis=-1, keepdims=True)
         out = jnp.dot(terms.astype(jnp.bfloat16), values, preferred_element_type=jnp.float32)
         return (out / total).astype(jnp.bfloat16)
@@ -503,7 +514,7 @@
     bf, f32 = jnp.bfloat16, jnp.float32
     vmem, smem = pl.BlockSpec(memory_space=pltpu.VMEM), pl.BlockSpec(memory_space=pltpu.SMEM)
     hbm = pl.BlockSpec(memory_space=pl.ANY)
-    copies = 9 * planes + 3 + 2 * seq_count + pb_count
+    copies = 10 * planes + 3 + 2 * seq_count + pb_count
     embedded, scores, grad, loss = pl.pallas_call(
         functools.partial(fused_kernel, seq_count, pb_count),
         out_shape=(

time: 73.1 us -> 73.8 us (level)
  no operation moved by 1% of the time
where the time goes in v4:
time: 73.8 us; the launch traced here: 73.6 us
  Pallas kernels  68.5 us (93%)
  between operations  3.05 us (4%)
  local copies, waits for them, and re-layouts  2 us (3%)
    pallas_call x1, Pallas kernels, fused(): pl.pallas_call(functools.partial(fused_kernel, seq_count, pb_count), out_...  68.5 us
    unnamed x7, local copies, waits for them, and re-layouts  2 us

profile of v4, /device:TPU:0, one launch (start us, length us, event | category | flops | bytes accessed | tf_op | source)
XLA Modules:
  0.0 73.6 jit_solution(8834032358265044754)
XLA Ops:
  1.3 68.5 %shard_map.138 = (bf16[256,2048]{1,0:T(8,128)(2,1)S(1)}, f32[1,16]{1,0:T(1,128)}, f32[1,16]{1,0:T(1,128)}, f32[1,1]{1,0:T(1,128)}) custom-call(s32[1]{0:T(128)S(6)} %copy.20.lengths_ref, s32[16]{0:T(128)} %groups_ref.1, bf16[256,2048]{1,0:T(8,128)(2,1)} %tokens_ref.1, f32[1,2048]{1,0:T(1,128)} %bitcast.5, f32[1,2048]{1,0:T(1,128)} %bitcast.6, ...), custom_call_target="tpu_custom_call" | custom-call | tf_op jit(solution)/shard_map/pallas_call | solution.py:518
  69.8 0.0 copy-start.1
  69.8 0.0 copy-start
  69.8 1.0 %copy.19 = bf16[256,2048]{1,0:T(8,128)(2,1)} copy(bf16[256,2048]{1,0:T(8,128)(2,1)S(1)} %get-tuple-element.12) | data formatting | bytes 2097152
  70.8 0.0 copy-done.1
  70.8 0.5 copy.21
  71.3 0.0 copy-done
  71.3 0.5 copy.22
Async XLA Ops:
  69.8 1.0 %copy-start.1 = (f32[1,16]{1,0:T(1,128)S(1)}, f32[1,16]{1,0:T(1,128)}, u32[]{:S(2)}) copy-start(f32[1,16]{1,0:T(1,128)} %get-tuple-element.21) | copy-start | bytes 196
  69.8 1.5 %copy-start = (f32[1,16]{1,0:T(1,128)S(1)}, f32[1,16]{1,0:T(1,128)}, u32[]{:S(2)}) copy-start(f32[1,16]{1,0:T(1,128)} %get-tuple-element.22) | copy-start | bytes 196
